TPU v7x, 512 devices: a whole 4x8x8 slice. The times are simulated.
512 devices in a mesh: sec: 8 (over y), rad: 16 (over z, x_hi), ax: 4 (over x_lo, core).
Axes of the slice: x: 4 (x_hi: 2, x_lo: 2; x = x_hi * 2 + x_lo), y: 8, z: 8, core: 2. Of those that a mesh axis runs over, the one named last changes fastest.
Arguments:
- state: float32 [5, 8, 1024, 2048], P(None, 'ax', 'rad', 'sec'), may hold values from -1.6 to 4, as said below
- coarsen: int32 [16], replicated, may hold values from 1 to 16, as said below
Outputs:
- tendency: float32 [5, 8, 1024, 2048], P(None, 'ax', 'rad', 'sec')
Inputs may be any that keep to these rules, and one draw needn't show every extreme that they name: `coarsen`: each entry is a power of two; cycle 0 takes 16 and cycle 16 - 1 takes 1. state[0] (density) lies in 0.6 to 1.4, the momenta in -1.6 to 1.6, state[4] (energy) in 2.5 to 4.0.
All inputs are finite; a program needn't handle non-finite values.
Results may differ from a plain program's by a relative error of at most 0.0003.
Values sent between devices are 32-bit elements; how exact they have to be, the bound alone decides.
A program may use at most 64 MiB of HBM per device.

v0:
```python
import math
import jax
import jax.numpy as jnp
from jax import lax
from jax.sharding import PartitionSpec as P

R_NEAR = 16
GAMMA = 1.4
KAPPA = 1.44


def padded_2(value, sides, width):
    for axis, dim in sides:
        size, length = (lax.axis_size(axis), value.shape[dim])
        up = [(i, (i + 1) % size) for i in range(size)]
        down = [(j, i) for i, j in up]
        last = lax.slice_in_dim(value, length - width, length, axis=dim)
        first = lax.slice_in_dim(value, 0, width, axis=dim)
        before = lax.ppermute(last, axis, up)
        after = lax.ppermute(first, axis, down)
        value = jnp.concatenate([before, value, after], axis=dim)
    return value


def spread(value, axis, root):
    mine = lax.axis_index(axis) == root
    return lax.psum(jnp.where(mine, value, jnp.zeros_like(value)), axis)


def body(state, coarsen):
    fields, planes, cycles_dev, cells_dev = state.shape
    sec_count = lax.axis_size("sec")
    rad_count = lax.axis_size("rad")
    ax_count = lax.axis_size("ax")
    sec_index = lax.axis_index("sec")
    rad_index = lax.axis_index("rad")
    ax_index = lax.axis_index("ax")
    total_cells = cells_dev * sec_count
    dtheta = 2.0 * math.pi / total_cells
    padded = padded_2(state, (("sec", 3), ("rad", 2), ("ax", 1)), 1)
    plane_pos = ax_index * planes + jnp.arange(-1, planes + 1, dtype=jnp.int32)
    cycle_pos = rad_index * cycles_dev + jnp.arange(-1, cycles_dev + 1, dtype=jnp.int32)
    inside_ax = ((plane_pos >= 0) & (plane_pos < planes * ax_count)).astype(jnp.float32)
    inside_rad = ((cycle_pos >= 0) & (cycle_pos < cycles_dev * rad_count)).astype(jnp.float32)
    ghost_plane = jnp.arange(planes + 2) % (planes + 1) == 0
    ghost_cycle = jnp.arange(cycles_dev + 2) % (cycles_dev + 1) == 0
    ghost_cell = jnp.arange(cells_dev + 2) % (cells_dev + 1) == 0
    ghosts = (
        ghost_plane.astype(jnp.int32)[:, None, None]
        + ghost_cycle.astype(jnp.int32)[None, :, None]
        + ghost_cell.astype(jnp.int32)[None, None, :]
    )
    corner = ghosts >= 2
    density = jnp.where(corner, 1.0, padded[0])
    mom_ax = padded[1]
    mom_rad = padded[2]
    mom_az = padded[3]
    energy = padded[4]
    vel_ax = mom_ax / density
    vel_rad = mom_rad / density
    vel_az = mom_az / density
    pressure = (GAMMA - 1.0) * (
        energy - 0.5 * (mom_ax * vel_ax + mom_rad * vel_rad + mom_az * vel_az)
    )
    radius_pad = cycle_pos.astype(jnp.float32) + 0.5
    flux_ax = jnp.stack(
        [
            mom_ax,
            mom_ax * vel_ax + pressure,
            mom_rad * vel_ax,
            mom_az * vel_ax,
            (energy + pressure) * vel_ax,
        ]
    )
    flux_ax = flux_ax * inside_ax[None, :, None, None]
    flux_rad = jnp.stack(
        [
            mom_rad,
            mom_ax * vel_rad,
            mom_rad * vel_rad + pressure,
            mom_az * vel_rad,
            (energy + pressure) * vel_rad,
        ]
    )
    flux_rad = flux_rad * (radius_pad * inside_rad)[None, None, :, None]
    flux_az = jnp.stack(
        [
            mom_az,
            mom_ax * vel_az,
            mom_rad * vel_az,
            mom_az * vel_az + pressure,
            (energy + pressure) * vel_az,
        ]
    )
    radius = radius_pad[1:-1][:, None]
    tendency = -(flux_ax[:, 2:, 1:-1, 1:-1] - flux_ax[:, :-2, 1:-1, 1:-1]) * 0.5
    tendency = (
        tendency - (flux_rad[:, 1:-1, 2:, 1:-1] - flux_rad[:, 1:-1, :-2, 1:-1]) * 0.5 / radius
    )
    tendency = tendency - (flux_az[:, 1:-1, 1:-1, 2:] - flux_az[:, 1:-1, 1:-1, :-2]) * 0.5 / (
        radius * dtheta
    )
    inner_press = pressure[1:-1, 1:-1, 1:-1]
    inner_mom_az = mom_az[1:-1, 1:-1, 1:-1]
    inner_mom_rad = mom_rad[1:-1, 1:-1, 1:-1]
    inner_vel_az = vel_az[1:-1, 1:-1, 1:-1]
    zero_part = jnp.zeros_like(inner_press)
    source = jnp.stack(
        [
            zero_part,
            zero_part,
            (inner_press + inner_mom_az * inner_vel_az) / radius,
            -(inner_mom_rad * inner_vel_az) / radius,
            zero_part,
        ]
    )
    tendency = tendency + source
    own_pos = sec_index * cells_dev + jnp.arange(cells_dev, dtype=jnp.int32)

    def kernel(cycle_factor, cycle_blocks, log_ratio, scale_const, columns):
        rows_coarse = own_pos // cycle_factor
        columns_coarse = columns // cycle_factor
        distance = ((rows_coarse[:, None] - columns_coarse[None, :]) % cycle_blocks).astype(
            jnp.float32
        )
        blocks_f = cycle_blocks.astype(jnp.float32)
        return (jnp.exp(distance * log_ratio) + jnp.exp((blocks_f - distance) * log_ratio)) / (
            scale_const * cycle_factor.astype(jnp.float32)
        )

    near_axis = tendency[:, :, :R_NEAR, :]
    cycle_lines = jnp.transpose(near_axis, (2, 0, 1, 3)).reshape(R_NEAR, fields * planes, cells_dev)
    shared = spread(cycle_lines, "rad", 0)
    per_device = R_NEAR // rad_count
    my_cycles = lax.dynamic_slice_in_dim(shared, rad_index * per_device, per_device, 0)
    selector = (rad_index * per_device + jnp.arange(per_device, dtype=jnp.int32))[
        :, None
    ] == jnp.arange(coarsen.shape[0], dtype=jnp.int32)[None, :]
    factor = jnp.sum(jnp.where(selector, coarsen[None, :], 0), axis=1)
    blocks = total_cells // factor
    factor_f = factor.astype(jnp.float32)
    stiffness = KAPPA / (factor_f * dtheta) ** 2
    inverse_half = 0.5 / stiffness
    one_minus = jnp.sqrt(inverse_half * (2.0 + inverse_half)) - inverse_half
    log_ratio = jnp.log1p(-one_minus)
    scale_const = (
        stiffness
        * one_minus
        * (2.0 - one_minus)
        / (1.0 - one_minus)
        * -jnp.expm1(blocks.astype(jnp.float32) * log_ratio)
    )
    portion = lax.all_gather(my_cycles, "sec", axis=2, tiled=True)
    columns = jnp.arange(portion.shape[2], dtype=jnp.int32)

    def per_cycle(cycle_item):
        lines_one, cycle_factor, cycle_blocks, cycle_log, cycle_scale = cycle_item
        table = kernel(cycle_factor, cycle_blocks, cycle_log, cycle_scale, columns)
        return jnp.einsum("lq,pq->lp", lines_one, table, precision=lax.Precision.HIGHEST)

    smoothed = lax.map(per_cycle, (portion, factor, blocks, log_ratio, scale_const))
    result = lax.all_gather(smoothed, "rad", axis=0, tiled=True)
    restored = jnp.transpose(result.reshape(R_NEAR, fields, planes, cells_dev), (1, 2, 0, 3))
    near_new = jnp.where(rad_index == 0, restored, near_axis)
    return jnp.concatenate([near_new, tendency[:, :, R_NEAR:, :]], axis=2)


def solution(mesh):
    return jax.shard_map(
        body,
        mesh=mesh,
        in_specs=(P(None, "ax", "rad", "sec"), P()),
        out_specs=P(None, "ax", "rad", "sec"),
        check_vma=False,
    )
```

profile of v0, /device:TPU:6, one launch (start us, length us, event | category | flops | bytes accessed | tf_op | source)
XLA Modules:
  0.0 309.1 jit_solution(6789559779002969412)
XLA Ops:
  6.5 1.3 fusion.47
  7.8 3.5 %collective-permute-start = (f32[5,2,64,1]{3,2,1,0:T(8,128)S(1)}, f32[5,2,64,1]{3,2,1,0:T(8,128)S(1)}, u32[]{:S(2)}, u32[]{:S(2)}) collective-permute-start(f32[5,2,64,1]{3,2,1,0:T(8,128)S(1)} %get-tuple-element.59), channel_id=1, source_target_pairs={{0,64},{64,128},{128,192},{192,256},{256,320},{320,384},{384,448},... | collective-permute-start | bytes 7688 | tf_op jit(solution)/shard_map/ppermute | solution.py:19
  11.3 3.8 %collective-permute-start.1 = (f32[5,2,64,1]{3,2,1,0:T(8,128)S(1)}, f32[5,2,64,1]{3,2,1,0:T(8,128)S(1)}, u32[]{:S(2)}, u32[]{:S(2)}) collective-permute-start(f32[5,2,64,1]{3,2,1,0:T(8,128)S(1)} %get-tuple-element.60), channel_id=1, source_target_pairs={{64,0},{128,64},{192,128},{256,192},{320,256},{384,320},{448,384},... | collective-permute-start | bytes 7688 | tf_op jit(solution)/shard_map/ppermute | solution.py:20
  15.2 1.4 fusion.44
  16.6 4.3 %collective-permute-done = f32[5,2,64,1]{3,2,1,0:T(8,128)S(1)} collective-permute-done((f32[5,2,64,1]{3,2,1,0:T(8,128)S(1)}, f32[5,2,64,1]{3,2,1,0:T(8,128)S(1)}, u32[]{:S(2)}, u32[]{:S(2)}) %collective-permute-start) | collective-permute-done | bytes 2592 | tf_op jit(solution)/shard_map/ppermute | solution.py:19
  20.9 1.5 collective-permute-done.1
  22.4 1.1 pad_maximum_fusion.5
  23.5 5.1 %collective-permute-start.2 = (f32[5,2,1,258]{3,2,1,0:T(1,128)S(1)}, f32[5,2,1,258]{3,2,1,0:T(1,128)S(1)}, u32[]{:S(2)}, u32[]{:S(2)}) collective-permute-start(f32[5,2,1,258]{3,2,1,0:T(1,128)S(1)} %get-tuple-element.53), channel_id=1, source_target_pairs={{0,4},{4,8},{8,12},{12,16},{16,20},{20,24},{24,28},{28,32},{32,36}... | collective-permute-start | bytes 30968 | tf_op jit(solution)/shard_map/ppermute | solution.py:19
  28.6 2.2 collective-permute-start.3
  30.9 5.8 %collective-permute-done.3 = f32[5,2,1,258]{3,2,1,0:T(1,128)S(1)} collective-permute-done((f32[5,2,1,258]{3,2,1,0:T(1,128)S(1)}, f32[5,2,1,258]{3,2,1,0:T(1,128)S(1)}, u32[]{:S(2)}, u32[]{:S(2)}) %collective-permute-start.3) | collective-permute-done | bytes 10352 | tf_op jit(solution)/shard_map/ppermute | solution.py:20
  37.2 0.5 copy.5
  37.7 1.9 collective-permute-start.4
  40.2 3.6 %collective-permute-start.5 = (f32[5,1,66,258]{3,1,2,0:T(1,128)S(1)}, f32[5,1,66,258]{3,1,2,0:T(1,128)S(1)}, u32[]{:S(2)}, u32[]{:S(2)}) collective-permute-start(f32[5,1,66,258]{3,1,2,0:T(1,128)S(1)} %copy.6), channel_id=1, source_target_pairs={{1,0},{2,1},{3,2},{0,3},{5,4},{6,5},{7,6},{4,7},{9,8},{10,9},{11,1... | collective-permute-start | bytes 1021688 | tf_op jit(solution)/shard_map/ppermute | solution.py:20
  44.7 6.0 %collective-permute-done.4 = f32[5,1,66,258]{3,1,2,0:T(1,128)S(1)} collective-permute-done((f32[5,1,66,258]{3,1,2,0:T(1,128)S(1)}, f32[5,1,66,258]{3,1,2,0:T(1,128)S(1)}, u32[]{:S(2)}, u32[]{:S(2)}) %collective-permute-start.4) | collective-permute-done | bytes 340592 | tf_op jit(solution)/shard_map/ppermute | solution.py:19
  53.6 1.1 fusion.19
  54.7 0.7 slice_select_fusion.1
  55.4 0.8 and_select_fusion
  58.5 0.8 add_select_fusion.1
  59.4 161.4 %all-reduce.2.cloned.1.call-done = f32[16,10,256]{2,0,1:T(8,128)} async-done(((f32[16,10,256]{2,0,1:T(8,128)}), f32[16,10,256]{2,0,1:T(8,128)}) %all-reduce.2.cloned.1.call-update) | async-done | bytes 163856 | tf_op jit(solution)/shard_map/psum | solution.py:27
  220.8 0.9 constant_dynamic-slice_fusion
  221.7 16.7 %all_gather.6 = f32[1,10,2048]{2,0,1:T(1,128)S(1)} all-gather(f32[1,10,256]{2,0,1:T(1,128)S(1)} %constant_dynamic-slice_fusion), channel_id=1, replica_groups=mesh['sec'=8,'rad'=16,'ax'=4] {'sec'}, dimensions={2}, use_global_device_ids=true | all-gather | bytes 92160 | tf_op jit(solution)/shard_map/all_gather | solution.py:153
  238.4 22.6 %fusion.7 = f32[1,10,256]{2,1,0:T(8,128)S(1)} fusion(f32[]{:T(128)S(6)} %mul.233, f32[]{:T(128)S(6)} %convert_element_type.66, f32[]{:T(128)} %bitcast.13, s32[]{:T(128)S(6)} %select_n.132, s32[2048]{0:T(1024)S(1)} %add_select_fusion.1, s32[256]{0:T(256)S(1)} %and_select_fusion, pred[]{:T(512)S(6)} %lt.63, f32[1,10,2048]{2,0,1:T(1,128)S(1)} %all_gather.6), kind=kOutput, calls=%fused_computation.10 | convolution fusion | flops 70254592 | bytes 101393 | tf_op jit(solution)/shard_map/while/body/eval_jaxpr/lq,pq->lp/dot_general | solution.py:159
  261.0 40.3 %all-gather.1 = f32[16,10,256]{2,1,0:T(8,128)S(1)} all-gather(f32[1,10,256]{2,1,0:T(8,128)S(1)} %fusion.7), channel_id=2, replica_groups=mesh['sec'=8,'rad'=16,'ax'=4] {'rad'}, dimensions={0}, use_global_device_ids=true | all-gather | bytes 174080 | tf_op jit(solution)/shard_map/all_gather | solution.py:162
  301.4 0.9 pad_maximum_fusion.2
  (38 shorter events, 4.4 us)
Async XLA Ops:
  6.5 30.1 %copy-start = (f32[5,2,64,256]{3,2,1,0:T(8,128)S(1)}, f32[5,2,64,256]{3,2,1,0:T(8,128)}, u32[]{:S(2)}) copy-start(f32[5,2,64,256]{3,2,1,0:T(8,128)} %param.2) | copy-start | bytes 1966084
  6.5 214.2 %all-reduce.2.cloned.1.call-start = ((), (), s32[]{:S(2)}) async-start(), calls=%async_computation | async-start | bytes 327680 | tf_op jit(solution)/shard_map/psum | solution.py:27
  7.8 13.1 %collective-permute-start = (f32[5,2,64,1]{3,2,1,0:T(8,128)S(1)}, f32[5,2,64,1]{3,2,1,0:T(8,128)S(1)}, u32[]{:S(2)}, u32[]{:S(2)}) collective-permute-start(f32[5,2,64,1]{3,2,1,0:T(8,128)S(1)} %get-tuple-element.59), channel_id=1, source_target_pairs={{0,64},{64,128},{128,192},{192,256},{256,320},{320,384},{384,448},... | collective-permute-start | bytes 7688 | tf_op jit(solution)/shard_map/ppermute | solution.py:19
  11.3 11.1 %collective-permute-start.1 = (f32[5,2,64,1]{3,2,1,0:T(8,128)S(1)}, f32[5,2,64,1]{3,2,1,0:T(8,128)S(1)}, u32[]{:S(2)}, u32[]{:S(2)}) collective-permute-start(f32[5,2,64,1]{3,2,1,0:T(8,128)S(1)} %get-tuple-element.60), channel_id=1, source_target_pairs={{64,0},{128,64},{192,128},{256,192},{320,256},{384,320},{448,384},... | collective-permute-start | bytes 7688 | tf_op jit(solution)/shard_map/ppermute | solution.py:20
  23.5 7.4 %collective-permute-start.2 = (f32[5,2,1,258]{3,2,1,0:T(1,128)S(1)}, f32[5,2,1,258]{3,2,1,0:T(1,128)S(1)}, u32[]{:S(2)}, u32[]{:S(2)}) collective-permute-start(f32[5,2,1,258]{3,2,1,0:T(1,128)S(1)} %get-tuple-element.53), channel_id=1, source_target_pairs={{0,4},{4,8},{8,12},{12,16},{16,20},{20,24},{24,28},{28,32},{32,36}... | collective-permute-start | bytes 30968 | tf_op jit(solution)/shard_map/ppermute | solution.py:19
  28.6 8.0 %collective-permute-start.3 = (f32[5,2,1,258]{3,2,1,0:T(1,128)S(1)}, f32[5,2,1,258]{3,2,1,0:T(1,128)S(1)}, u32[]{:S(2)}, u32[]{:S(2)}) collective-permute-start(f32[5,2,1,258]{3,2,1,0:T(1,128)S(1)} %get-tuple-element.54), channel_id=1, source_target_pairs={{4,0},{8,4},{12,8},{16,12},{20,16},{24,20},{28,24},{32,28},{36,32}... | collective-permute-start | bytes 30968 | tf_op jit(solution)/shard_map/ppermute | solution.py:20
  37.7 13.0 %collective-permute-start.4 = (f32[5,1,66,258]{3,1,2,0:T(1,128)S(1)}, f32[5,1,66,258]{3,1,2,0:T(1,128)S(1)}, u32[]{:S(2)}, u32[]{:S(2)}) collective-permute-start(f32[5,1,66,258]{3,1,2,0:T(1,128)S(1)} %copy.5), channel_id=1, source_target_pairs={{0,1},{1,2},{2,3},{3,0},{4,5},{5,6},{6,7},{7,4},{8,9},{9,10},{10,1... | collective-permute-start | bytes 1021688 | tf_op jit(solution)/shard_map/ppermute | solution.py:19
  40.2 10.7 %collective-permute-start.5 = (f32[5,1,66,258]{3,1,2,0:T(1,128)S(1)}, f32[5,1,66,258]{3,1,2,0:T(1,128)S(1)}, u32[]{:S(2)}, u32[]{:S(2)}) collective-permute-start(f32[5,1,66,258]{3,1,2,0:T(1,128)S(1)} %copy.6), channel_id=1, source_target_pairs={{1,0},{2,1},{3,2},{0,3},{5,4},{6,5},{7,6},{4,7},{9,8},{10,9},{11,1... | collective-permute-start | bytes 1021688 | tf_op jit(solution)/shard_map/ppermute | solution.py:20
Sparse Core Ops, SparseCore 0:
  55.5 165.2 all-reduce.1
where the time goes:
time: 310 us; the launch traced here: 309 us
  waiting for transfers between devices  179 us (58%)
  blocking collectives  57 us (18%)
  matrix products  22.6 us (7%)
  starting transfers between devices  20.2 us (7%)
  between operations  16.7 us (5%)
  other arithmetic  9.79 us (3%)
  local copies, waits for them, and re-layouts  3.82 us (1%)
    psum x1, waiting for transfers between devices, spread(): return lax.psum(jnp.where(mine, value, jnp.zeros_like(value)), axis)  161 us
    all_gather x1, blocking collectives, body(): result = lax.all_gather(smoothed, 'rad', axis=0, tiled=True)  40.3 us
    dot_general x1, matrix products, per_cycle(): jnp.einsum('lq,pq->lp', lines_one, table, precision=lax.Precision.HIGHEST)  22.6 us
    all_gather x1, blocking collectives, body(): portion = lax.all_gather(my_cycles, 'sec', axis=2, tiled=True)  16.7 us
    ppermute x3, starting transfers between devices, padded_2(): before = lax.ppermute(last, axis, up)  10.5 us
    ppermute x3, waiting for transfers between devices, padded_2(): before = lax.ppermute(last, axis, up)  10.3 us
    ppermute x3, starting transfers between devices, padded_2(): after = lax.ppermute(first, axis, down)  9.68 us
    ppermute x3, waiting for transfers between devices, padded_2(): after = lax.ppermute(first, axis, down)  7.38 us
  transfers between devices with their start and end apart: 7, of which 6 were waited for; matrix products, arithmetic and copies ran while one was open for 1% of the time, Pallas kernels for 0%

commit v1 on v0

--- a/solution.py
+++ b/solution.py
@@ -150,7 +150,13 @@
         / (1.0 - one_minus)
         * -jnp.expm1(blocks.astype(jnp.float32) * log_ratio)
     )
-    portion = lax.all_gather(my_cycles, "sec", axis=2, tiled=True)
+    devices = lax.axis_size("sec")
+    held, pieces = (my_cycles, [my_cycles])
+    for _ in range(devices - 1):
+        held = lax.ppermute(held, "sec", [(i_2, (i_2 + 1) % devices) for i_2 in range(devices)])
+        pieces.insert(0, held)
+    line = jnp.concatenate(pieces, axis=2)
+    portion = jnp.roll(line, (lax.axis_index("sec") + 1) * my_cycles.shape[2], axis=2)
     columns = jnp.arange(portion.shape[2], dtype=jnp.int32)
 
     def per_cycle(cycle_item):

time: 310 us -> 343 us (1.11)
  waiting for transfers between devices: 179 us -> 212 us
  blocking collectives: 57 us -> 40.3 us
  starting transfers between devices: 20.2 us -> 35.5 us
    ppermute x0 -> x7, waiting for transfers between devices: none -> 26.9 us  [body(): lax.ppermute(held, 'sec', [(i_2, (i_2 + 1) % devices) for i_2 in range(de...]
    all_gather x1 -> x0, blocking collectives: 16.7 us -> none  [body(): portion = lax.all_gather(my_cycles, 'sec', axis=2, tiled=True)]
    ppermute x0 -> x7, starting transfers between devices: none -> 15.3 us  [body(): lax.ppermute(held, 'sec', [(i_2, (i_2 + 1) % devices) for i_2 in range(de...]
    psum x1, waiting for transfers between devices: 161 us -> 165 us  [spread(): return lax.psum(jnp.where(mine, value, jnp.zeros_like(value)), axis)]
  transfers between devices with their start and end apart: 7 -> 14, of which waited for: 6 -> 13; matrix products, arithmetic and copies ran while one was open for 1% -> 1% of each run, Pallas kernels for 0% -> 0%
where the time goes in v1:
time: 343 us; the launch traced here: 342 us
  waiting for transfers between devices  212 us (62%)
  blocking collectives  40.3 us (12%)
  starting transfers between devices  35.5 us (10%)
  matrix products  22.6 us (7%)
  between operations  16.6 us (5%)
  other arithmetic  8.94 us (3%)
  local copies, waits for them, and re-layouts  5.82 us (2%)
    psum x1, waiting for transfers between devices, spread(): return lax.psum(jnp.where(mine, value, jnp.zeros_like(value)), axis)  165 us
    all_gather x1, blocking collectives, body(): result = lax.all_gather(smoothed, 'rad', axis=0, tiled=True)  40.3 us
    ppermute x7, waiting for transfers between devices, body(): lax.ppermute(held, 'sec', [(i_2, (i_2 + 1) % devices) for i_2 in range(de...  26.9 us
    dot_general x1, matrix products, per_cycle(): jnp.einsum('lq,pq->lp', lines_one, table, precision=lax.Precision.HIGHEST)  22.6 us
    ppermute x7, starting transfers between devices, body(): lax.ppermute(held, 'sec', [(i_2, (i_2 + 1) % devices) for i_2 in range(de...  15.3 us
    ppermute x3, waiting for transfers between devices, padded_2(): before = lax.ppermute(last, axis, up)  12.4 us
    ppermute x3, starting transfers between devices, padded_2(): before = lax.ppermute(last, axis, up)  10.5 us
    ppermute x3, starting transfers between devices, padded_2(): after = lax.ppermute(first, axis, down)  9.68 us
  transfers between devices with their start and end apart: 14, of which 13 were waited for; matrix products, arithmetic and copies ran while one was open for 1% of the time, Pallas kernels for 0%

profile of v1, /device:TPU:6, one launch (start us, length us, event | category | flops | bytes accessed | tf_op | source)
XLA Modules:
  0.0 341.8 jit_solution(14723761056038695276)
XLA Ops:
  7.8 3.5 %collective-permute-start = (f32[5,2,64,1]{3,2,1,0:T(8,128)S(1)}, f32[5,2,64,1]{3,2,1,0:T(8,128)S(1)}, u32[]{:S(2)}, u32[]{:S(2)}) collective-permute-start(f32[5,2,64,1]{3,2,1,0:T(8,128)S(1)} %get-tuple-element.59), channel_id=1, source_target_pairs={{0,64},{64,128},{128,192},{192,256},{256,320},{320,384},{384,448},... | collective-permute-start | bytes 7688 | tf_op jit(solution)/shard_map/ppermute | solution.py:19
  11.3 3.8 %collective-permute-start.1 = (f32[5,2,64,1]{3,2,1,0:T(8,128)S(1)}, f32[5,2,64,1]{3,2,1,0:T(8,128)S(1)}, u32[]{:S(2)}, u32[]{:S(2)}) collective-permute-start(f32[5,2,64,1]{3,2,1,0:T(8,128)S(1)} %get-tuple-element.60), channel_id=1, source_target_pairs={{64,0},{128,64},{192,128},{256,192},{320,256},{384,320},{448,384},... | collective-permute-start | bytes 7688 | tf_op jit(solution)/shard_map/ppermute | solution.py:20
  15.3 5.6 %collective-permute-done = f32[5,2,64,1]{3,2,1,0:T(8,128)S(1)} collective-permute-done((f32[5,2,64,1]{3,2,1,0:T(8,128)S(1)}, f32[5,2,64,1]{3,2,1,0:T(8,128)S(1)}, u32[]{:S(2)}, u32[]{:S(2)}) %collective-permute-start) | collective-permute-done | bytes 2592 | tf_op jit(solution)/shard_map/ppermute | solution.py:19
  23.5 5.1 %collective-permute-start.2 = (f32[5,2,1,258]{3,2,1,0:T(1,128)S(1)}, f32[5,2,1,258]{3,2,1,0:T(1,128)S(1)}, u32[]{:S(2)}, u32[]{:S(2)}) collective-permute-start(f32[5,2,1,258]{3,2,1,0:T(1,128)S(1)} %get-tuple-element.53), channel_id=1, source_target_pairs={{0,4},{4,8},{8,12},{12,16},{16,20},{20,24},{24,28},{28,32},{32,36}... | collective-permute-start | bytes 30968 | tf_op jit(solution)/shard_map/ppermute | solution.py:19
  28.6 2.2 collective-permute-start.3
  30.9 5.8 %collective-permute-done.3 = f32[5,2,1,258]{3,2,1,0:T(1,128)S(1)} collective-permute-done((f32[5,2,1,258]{3,2,1,0:T(1,128)S(1)}, f32[5,2,1,258]{3,2,1,0:T(1,128)S(1)}, u32[]{:S(2)}, u32[]{:S(2)}) %collective-permute-start.3) | collective-permute-done | bytes 10352 | tf_op jit(solution)/shard_map/ppermute | solution.py:20
  37.7 1.9 collective-permute-start.4
  40.2 3.6 %collective-permute-start.5 = (f32[5,1,66,258]{3,1,2,0:T(1,128)S(1)}, f32[5,1,66,258]{3,1,2,0:T(1,128)S(1)}, u32[]{:S(2)}, u32[]{:S(2)}) collective-permute-start(f32[5,1,66,258]{3,1,2,0:T(1,128)S(1)} %copy.6), channel_id=1, source_target_pairs={{1,0},{2,1},{3,2},{0,3},{5,4},{6,5},{7,6},{4,7},{9,8},{10,9},{11,1... | collective-permute-start | bytes 1021688 | tf_op jit(solution)/shard_map/ppermute | solution.py:20
  44.0 6.7 %collective-permute-done.4 = f32[5,1,66,258]{3,1,2,0:T(1,128)S(1)} collective-permute-done((f32[5,1,66,258]{3,1,2,0:T(1,128)S(1)}, f32[5,1,66,258]{3,1,2,0:T(1,128)S(1)}, u32[]{:S(2)}, u32[]{:S(2)}) %collective-permute-start.4) | collective-permute-done | bytes 340592 | tf_op jit(solution)/shard_map/ppermute | solution.py:19
  55.4 165.4 %all-reduce.2.cloned.1.call-done = f32[16,10,256]{2,0,1:T(8,128)} async-done(((f32[16,10,256]{2,0,1:T(8,128)}), f32[16,10,256]{2,0,1:T(8,128)}) %all-reduce.2.cloned.1.call-update) | async-done | bytes 163856 | tf_op jit(solution)/shard_map/psum | solution.py:27
  221.7 3.4 collective-permute-start.6
  225.1 3.4 collective-permute-done.6
  228.5 2.2 collective-permute-start.7
  230.6 4.6 %collective-permute-done.7 = f32[1,10,256]{2,0,1:T(1,128)S(1)} collective-permute-done((f32[1,10,256]{2,0,1:T(1,128)S(1)}, f32[1,10,256]{2,0,1:T(1,128)S(1)}, u32[]{:S(2)}, u32[]{:S(2)}) %collective-permute-start.7) | collective-permute-done | bytes 10272 | tf_op jit(solution)/shard_map/ppermute | solution.py:156
  235.2 1.9 collective-permute-start.8
  237.1 4.8 %collective-permute-done.8 = f32[1,10,256]{2,0,1:T(1,128)S(1)} collective-permute-done((f32[1,10,256]{2,0,1:T(1,128)S(1)}, f32[1,10,256]{2,0,1:T(1,128)S(1)}, u32[]{:S(2)}, u32[]{:S(2)}) %collective-permute-start.8) | collective-permute-done | bytes 10272 | tf_op jit(solution)/shard_map/ppermute | solution.py:156
  242.0 1.9 collective-permute-start.9
  243.9 4.8 %collective-permute-done.9 = f32[1,10,256]{2,0,1:T(1,128)S(1)} collective-permute-done((f32[1,10,256]{2,0,1:T(1,128)S(1)}, f32[1,10,256]{2,0,1:T(1,128)S(1)}, u32[]{:S(2)}, u32[]{:S(2)}) %collective-permute-start.9) | collective-permute-done | bytes 10272 | tf_op jit(solution)/shard_map/ppermute | solution.py:156
  248.8 1.9 collective-permute-start.10
  252.0 3.6 %collective-permute-done.10 = f32[1,10,256]{2,0,1:T(1,128)S(1)} collective-permute-done((f32[1,10,256]{2,0,1:T(1,128)S(1)}, f32[1,10,256]{2,0,1:T(1,128)S(1)}, u32[]{:S(2)}, u32[]{:S(2)}) %collective-permute-start.10) | collective-permute-done | bytes 10272 | tf_op jit(solution)/shard_map/ppermute | solution.py:156
  258.2 4.1 %collective-permute-done.11 = f32[1,10,256]{2,0,1:T(1,128)S(1)} collective-permute-done((f32[1,10,256]{2,0,1:T(1,128)S(1)}, f32[1,10,256]{2,0,1:T(1,128)S(1)}, u32[]{:S(2)}, u32[]{:S(2)}) %collective-permute-start.11) | collective-permute-done | bytes 10272 | tf_op jit(solution)/shard_map/ppermute | solution.py:156
  262.3 2.1 collective-permute-start.12
  271.1 22.6 %fusion.7 = f32[1,10,256]{2,1,0:T(8,128)S(1)} fusion(f32[]{:T(128)S(6)} %mul.237, f32[]{:T(128)S(6)} %convert_element_type.66, f32[]{:T(128)} %bitcast.13, s32[]{:T(128)S(6)} %select_n.146, s32[2048]{0:T(1024)S(1)} %add_select_fusion.1, s32[256]{0:T(256)S(1)} %and_select_fusion, pred[]{:T(512)S(6)} %lt.77, f32[1,10,2048]{2,0,1:T(1,128)S(1)} %constant_dynamic-slice_fusion), kind=kOutput, calls=%fused_computation.10 | convolution fusion | flops 70254592 | bytes 101393 | tf_op jit(solution)/shard_map/while/body/eval_jaxpr/lq,pq->lp/dot_general | solution.py:165
  293.7 40.3 %all-gather.1 = f32[16,10,256]{2,1,0:T(8,128)S(1)} all-gather(f32[1,10,256]{2,1,0:T(8,128)S(1)} %fusion.7), channel_id=2, replica_groups=mesh['sec'=8,'rad'=16,'ax'=4] {'rad'}, dimensions={0}, use_global_device_ids=true | all-gather | bytes 174080 | tf_op jit(solution)/shard_map/all_gather | solution.py:168
  (70 shorter events, 19.9 us)
Async XLA Ops:
  6.5 30.1 %copy-start = (f32[5,2,64,256]{3,2,1,0:T(8,128)S(1)}, f32[5,2,64,256]{3,2,1,0:T(8,128)}, u32[]{:S(2)}) copy-start(f32[5,2,64,256]{3,2,1,0:T(8,128)} %param.2) | copy-start | bytes 1966084
  6.5 214.2 %all-reduce.2.cloned.1.call-start = ((), (), s32[]{:S(2)}) async-start(), calls=%async_computation | async-start | bytes 327680 | tf_op jit(solution)/shard_map/psum | solution.py:27
  7.8 13.1 %collective-permute-start = (f32[5,2,64,1]{3,2,1,0:T(8,128)S(1)}, f32[5,2,64,1]{3,2,1,0:T(8,128)S(1)}, u32[]{:S(2)}, u32[]{:S(2)}) collective-permute-start(f32[5,2,64,1]{3,2,1,0:T(8,128)S(1)} %get-tuple-element.59), channel_id=1, source_target_pairs={{0,64},{64,128},{128,192},{192,256},{256,320},{320,384},{384,448},... | collective-permute-start | bytes 7688 | tf_op jit(solution)/shard_map/ppermute | solution.py:19
  11.3 11.1 %collective-permute-start.1 = (f32[5,2,64,1]{3,2,1,0:T(8,128)S(1)}, f32[5,2,64,1]{3,2,1,0:T(8,128)S(1)}, u32[]{:S(2)}, u32[]{:S(2)}) collective-permute-start(f32[5,2,64,1]{3,2,1,0:T(8,128)S(1)} %get-tuple-element.60), channel_id=1, source_target_pairs={{64,0},{128,64},{192,128},{256,192},{320,256},{384,320},{448,384},... | collective-permute-start | bytes 7688 | tf_op jit(solution)/shard_map/ppermute | solution.py:20
  23.5 7.4 %collective-permute-start.2 = (f32[5,2,1,258]{3,2,1,0:T(1,128)S(1)}, f32[5,2,1,258]{3,2,1,0:T(1,128)S(1)}, u32[]{:S(2)}, u32[]{:S(2)}) collective-permute-start(f32[5,2,1,258]{3,2,1,0:T(1,128)S(1)} %get-tuple-element.53), channel_id=1, source_target_pairs={{0,4},{4,8},{8,12},{12,16},{16,20},{20,24},{24,28},{28,32},{32,36}... | collective-permute-start | bytes 30968 | tf_op jit(solution)/shard_map/ppermute | solution.py:19
  28.6 8.0 %collective-permute-start.3 = (f32[5,2,1,258]{3,2,1,0:T(1,128)S(1)}, f32[5,2,1,258]{3,2,1,0:T(1,128)S(1)}, u32[]{:S(2)}, u32[]{:S(2)}) collective-permute-start(f32[5,2,1,258]{3,2,1,0:T(1,128)S(1)} %get-tuple-element.54), channel_id=1, source_target_pairs={{4,0},{8,4},{12,8},{16,12},{20,16},{24,20},{28,24},{32,28},{36,32}... | collective-permute-start | bytes 30968 | tf_op jit(solution)/shard_map/ppermute | solution.py:20
  37.7 13.0 %collective-permute-start.4 = (f32[5,1,66,258]{3,1,2,0:T(1,128)S(1)}, f32[5,1,66,258]{3,1,2,0:T(1,128)S(1)}, u32[]{:S(2)}, u32[]{:S(2)}) collective-permute-start(f32[5,1,66,258]{3,1,2,0:T(1,128)S(1)} %copy.5), channel_id=1, source_target_pairs={{0,1},{1,2},{2,3},{3,0},{4,5},{5,6},{6,7},{7,4},{8,9},{9,10},{10,1... | collective-permute-start | bytes 1021688 | tf_op jit(solution)/shard_map/ppermute | solution.py:19
  40.2 10.7 %collective-permute-start.5 = (f32[5,1,66,258]{3,1,2,0:T(1,128)S(1)}, f32[5,1,66,258]{3,1,2,0:T(1,128)S(1)}, u32[]{:S(2)}, u32[]{:S(2)}) collective-permute-start(f32[5,1,66,258]{3,1,2,0:T(1,128)S(1)} %copy.6), channel_id=1, source_target_pairs={{1,0},{2,1},{3,2},{0,3},{5,4},{6,5},{7,6},{4,7},{9,8},{10,9},{11,1... | collective-permute-start | bytes 1021688 | tf_op jit(solution)/shard_map/ppermute | solution.py:20
  53.6 197.1 %copy-start.1 = (s32[16]{0:T(128)S(1)}, s32[16]{0:T(128)}, u32[]{:S(2)}) copy-start(s32[16]{0:T(128)} %param.3) | copy-start | bytes 196
  221.7 6.8 %collective-permute-start.6 = (f32[1,10,256]{2,0,1:T(1,128)S(1)}, f32[1,10,256]{2,0,1:T(1,128)S(1)}, u32[]{:S(2)}, u32[]{:S(2)}) collective-permute-start(f32[1,10,256]{2,0,1:T(1,128)S(1)} %constant_dynamic-slice_fusion.1), channel_id=1, source_target_pairs={{0,64},{64,128},{128,192},{192,256},{256,320},{320,384},{384,448},... | collective-permute-start | bytes 30728 | tf_op jit(solution)/shard_map/ppermute | solution.py:156
  228.5 6.8 %collective-permute-start.7 = (f32[1,10,256]{2,0,1:T(1,128)S(1)}, f32[1,10,256]{2,0,1:T(1,128)S(1)}, u32[]{:S(2)}, u32[]{:S(2)}) collective-permute-start(f32[1,10,256]{2,0,1:T(1,128)S(1)} %collective-permute-done.6), channel_id=1, source_target_pairs={{0,64},{64,128},{128,192},{192,256},{256,320},{320,384},{384,448},... | collective-permute-start | bytes 30728 | tf_op jit(solution)/shard_map/ppermute | solution.py:156
  235.2 6.8 %collective-permute-start.8 = (f32[1,10,256]{2,0,1:T(1,128)S(1)}, f32[1,10,256]{2,0,1:T(1,128)S(1)}, u32[]{:S(2)}, u32[]{:S(2)}) collective-permute-start(f32[1,10,256]{2,0,1:T(1,128)S(1)} %collective-permute-done.7), channel_id=1, source_target_pairs={{0,64},{64,128},{128,192},{192,256},{256,320},{320,384},{384,448},... | collective-permute-start | bytes 30728 | tf_op jit(solution)/shard_map/ppermute | solution.py:156
  242.0 6.8 %collective-permute-start.9 = (f32[1,10,256]{2,0,1:T(1,128)S(1)}, f32[1,10,256]{2,0,1:T(1,128)S(1)}, u32[]{:S(2)}, u32[]{:S(2)}) collective-permute-start(f32[1,10,256]{2,0,1:T(1,128)S(1)} %collective-permute-done.8), channel_id=1, source_target_pairs={{0,64},{64,128},{128,192},{192,256},{256,320},{320,384},{384,448},... | collective-permute-start | bytes 30728 | tf_op jit(solution)/shard_map/ppermute | solution.py:156
  248.8 6.8 %collective-permute-start.10 = (f32[1,10,256]{2,0,1:T(1,128)S(1)}, f32[1,10,256]{2,0,1:T(1,128)S(1)}, u32[]{:S(2)}, u32[]{:S(2)}) collective-permute-start(f32[1,10,256]{2,0,1:T(1,128)S(1)} %collective-permute-done.9), channel_id=1, source_target_pairs={{0,64},{64,128},{128,192},{192,256},{256,320},{320,384},{384,448},... | collective-permute-start | bytes 30728 | tf_op jit(solution)/shard_map/ppermute | solution.py:156
  255.5 6.8 %collective-permute-start.11 = (f32[1,10,256]{2,0,1:T(1,128)S(1)}, f32[1,10,256]{2,0,1:T(1,128)S(1)}, u32[]{:S(2)}, u32[]{:S(2)}) collective-permute-start(f32[1,10,256]{2,0,1:T(1,128)S(1)} %collective-permute-done.10), channel_id=1, source_target_pairs={{0,64},{64,128},{128,192},{192,256},{256,320},{320,384},{384,448},... | collective-permute-start | bytes 30728 | tf_op jit(solution)/shard_map/ppermute | solution.py:156
  262.3 6.8 %collective-permute-start.12 = (f32[1,10,256]{2,0,1:T(1,128)S(1)}, f32[1,10,256]{2,0,1:T(1,128)S(1)}, u32[]{:S(2)}, u32[]{:S(2)}) collective-permute-start(f32[1,10,256]{2,0,1:T(1,128)S(1)} %collective-permute-done.11), channel_id=1, source_target_pairs={{0,64},{64,128},{128,192},{192,256},{256,320},{320,384},{384,448},... | collective-permute-start | bytes 30728 | tf_op jit(solution)/shard_map/ppermute | solution.py:156
Sparse Core Ops, SparseCore 0:
  55.5 165.2 all-reduce.1
